TPU v7x, 256 devices: a whole 4x4x8 slice. The times are simulated.
256 devices in a mesh: fsdp: 64 (over z_lo, y, x), seq: 4 (over z_hi, core).
Axes of the slice: x: 4, y: 4, z: 8 (z_hi: 2, z_lo: 4; z = z_hi * 4 + z_lo), core: 2. Of those that a mesh axis runs over, the one named last changes fastest.
Arguments:
- queries: bfloat16 [64, 768, 2048], P('fsdp', 'seq'), may hold values from -8 to 8, as said below
- keys: bfloat16 [64, 768, 2048], P('fsdp', 'seq'), may hold values from -8 to 8, as said below
- values: bfloat16 [64, 768, 2048], P('fsdp', 'seq'), may hold values from -6 to 6
- out_grad: bfloat16 [64, 768, 4096], P('fsdp', 'seq'), may hold values from -3 to 3
- out_weight: bfloat16 [2048, 4096], P('fsdp', 'seq'), may hold values from -0.125 to 0.125
- time_gate: float32 [32, 4096], replicated, may hold values from -3 to 3
- speaker_gate: float32 [64, 4096], replicated, may hold values from -3 to 3
- time_steps: int32 [64], replicated, may hold values from 0 to 31
- speakers: int32 [64], replicated, may hold values from 0 to 63
- lengths: int32 [64], replicated, may hold values from 384 to 768, as said below
Outputs:
- query_grad: bfloat16 [64, 768, 2048], P('fsdp', 'seq')
- key_grad: bfloat16 [64, 768, 2048], P('fsdp', 'seq')
- value_grad: bfloat16 [64, 768, 2048], P('fsdp', 'seq')
- time_gate_grad: float32 [32, 4096], replicated
- speaker_gate_grad: float32 [64, 4096], replicated
Inputs may be any that keep to these rules, and one draw needn't show every extreme that they name: `queries`: queries lie within this range. `keys`: keys lie within this range. `lengths`: some clip has all 768 frames live.
All inputs are finite; a program needn't handle non-finite values.
Results may differ from a plain program's by a relative error of at most 0.038.
Values may be sent and summed in bfloat16 or wider, within the bound.
A program may use at most 128 MiB of HBM per device.

v0:
```python
import jax
import jax.numpy as jnp
from jax import lax
from jax.sharding import PartitionSpec as P

HEADS = 16
HEAD_DIM = 128
TT = 32
SPK = 64


def shards(
    queries,
    keys,
    values,
    out_grad,
    out_weight,
    time_gate,
    speaker_gate,
    time_steps,
    speakers,
    lengths,
):
    query = queries[0]
    grad_out = out_grad[0]
    rows, width = query.shape
    scale = HEAD_DIM ** (-0.5)
    clip = lax.axis_index("fsdp")
    my_time = time_steps[clip]
    my_speaker = speakers[clip]
    my_length = lengths[clip]
    gate = lax.dynamic_index_in_dim(time_gate, my_time, 0, False) + lax.dynamic_index_in_dim(
        speaker_gate, my_speaker, 0, False
    )
    key_all, value_all = (
        lax.all_gather(keys, "seq", axis=1, tiled=True),
        lax.all_gather(values, "seq", axis=1, tiled=True),
    )
    frames = key_all.shape[1]
    query_h = query.reshape(rows, HEADS, HEAD_DIM)
    key_h = key_all[0].reshape(frames, HEADS, HEAD_DIM)
    value_h = value_all[0].reshape(frames, HEADS, HEAD_DIM)
    live = jnp.arange(frames) < my_length
    scores = jnp.einsum("qhd,khd->hqk", query_h, key_h, preferred_element_type=jnp.float32) * scale
    scores = jnp.where(live[None, None, :], scores, -1e30)
    top = jnp.max(scores, axis=-1, keepdims=True)
    expo = jnp.exp(scores - top)
    probs = expo / jnp.sum(expo, axis=-1, keepdims=True)
    probs_low = probs.astype(jnp.bfloat16)
    heads_out = (
        jnp.einsum("hqk,khd->qhd", probs_low, value_h, preferred_element_type=jnp.float32)
        .reshape(rows, width)
        .astype(jnp.bfloat16)
    )
    weight_full = lax.all_gather(
        lax.all_gather(out_weight, "seq", axis=1, tiled=True), "fsdp", axis=0, tiled=True
    )
    proj = jnp.dot(heads_out, weight_full, preferred_element_type=jnp.float32)
    gate_grad = lax.psum(jnp.sum(grad_out.astype(jnp.float32) * proj, axis=0), "seq")
    scaled = (grad_out.astype(jnp.float32) * gate[None, :]).astype(jnp.bfloat16)
    heads_grad = lax.dot_general(
        scaled, weight_full, (((1,), (1,)), ((), ())), preferred_element_type=jnp.float32
    ).astype(jnp.bfloat16)
    grad_h = heads_grad.reshape(rows, HEADS, HEAD_DIM)
    out_h = heads_out.reshape(rows, HEADS, HEAD_DIM)
    delta = jnp.sum(grad_h.astype(jnp.float32) * out_h.astype(jnp.float32), axis=-1).T
    prob_grad = jnp.einsum("qhd,khd->hqk", grad_h, value_h, preferred_element_type=jnp.float32)
    score_grad = (probs * (prob_grad - delta[:, :, None])).astype(jnp.bfloat16)
    query_grad = (
        (jnp.einsum("hqk,khd->qhd", score_grad, key_h, preferred_element_type=jnp.float32) * scale)
        .reshape(rows, width)
        .astype(jnp.bfloat16)
    )
    key_term = (
        jnp.einsum("hqk,qhd->khd", score_grad, query_h, preferred_element_type=jnp.float32) * scale
    ).reshape(frames, width)
    value_term = jnp.einsum(
        "hqk,qhd->khd", probs_low, grad_h, preferred_element_type=jnp.float32
    ).reshape(frames, width)
    key_sum, value_sum = (
        lax.psum_scatter(
            key_term.astype(jnp.bfloat16), "seq", scatter_dimension=0, tiled=True
        ).astype(jnp.float32),
        lax.psum_scatter(
            value_term.astype(jnp.bfloat16), "seq", scatter_dimension=0, tiled=True
        ).astype(jnp.float32),
    )
    key_grad = key_sum.astype(jnp.bfloat16)
    value_grad = value_sum.astype(jnp.bfloat16)
    time_hot = (jnp.arange(TT) == my_time).astype(jnp.float32)[:, None] * gate_grad[None, :]
    speaker_hot = (jnp.arange(SPK) == my_speaker).astype(jnp.float32)[:, None] * gate_grad[None, :]
    time_gate_grad, speaker_gate_grad = lax.psum((time_hot, speaker_hot), "fsdp")
    return (query_grad[None], key_grad[None], value_grad[None], time_gate_grad, speaker_gate_grad)


def solution(mesh):
    in_specs = (
        P("fsdp", "seq", None),
        P("fsdp", "seq", None),
        P("fsdp", "seq", None),
        P("fsdp", "seq", None),
        P("fsdp", "seq"),
        P(),
        P(),
        P(),
        P(),
        P(),
    )
    out_specs = (P("fsdp", "seq", None), P("fsdp", "seq", None), P("fsdp", "seq", None), P(), P())
    return jax.shard_map(shards, mesh=mesh, in_specs=in_specs, out_specs=out_specs, check_vma=False)
```

profile of v0, /device:TPU:71, one launch (start us, length us, event | category | flops | bytes accessed | tf_op | source)
XLA Modules:
  0.0 1406.8 jit_solution(11125948167713118738)
XLA Ops:
  7.2 0.0 all-gather.4.cloned.1.call-start
  7.2 0.7 all-gather.4.cloned.1.call-update
  7.9 0.0 all-gather.8.cloned.1.call-start
  7.9 0.7 all-gather.8.cloned.1.call-update
  8.6 0.0 all-gather.6.cloned.1.call-start
  8.7 13.2 all_gather.13
  21.9 0.0 all-gather.6.cloned.1.call-update
  21.9 0.0 all-reduce.3.cloned.1.call-start
  22.0 1.2 dynamic_slice.20
  24.5 1.2 dynamic_slice.18
  27.1 1.2 dynamic_slice.17
  28.3 2.2 copy.58
  31.8 0.6 compare_convert_fusion
  32.5 0.7 compare_convert_fusion.1
  33.1 0.7 iota_compare_fusion
  33.8 1.0 dynamic-slice_add_fusion
  34.8 30.1 %all-gather.4.cloned.1.call-done = bf16[1,768,2048]{2,1,0:T(8,128)(2,1)} async-done(((bf16[1,192,2048]{2,1,0:T(8,128)(2,1)}), bf16[1,768,2048]{2,1,0:T(8,128)(2,1)}) %all-gather.4.cloned.1.call-update) | async-done | bytes 3145744 | tf_op jit(solution)/shard_map/all_gather | solution.py:36
  64.9 3.2 copy.37
  68.1 49.7 %all-gather.8.cloned.1.call-done = bf16[1,768,2048]{2,1,0:T(8,128)(2,1)} async-done(((bf16[1,192,2048]{2,1,0:T(8,128)(2,1)}), bf16[1,768,2048]{2,1,0:T(8,128)(2,1)}) %all-gather.8.cloned.1.call-update) | async-done | bytes 3145744 | tf_op jit(solution)/shard_map/all_gather | solution.py:37
  117.8 4.7 copy.40
  122.5 2.5 fusion.20
  125.0 5.5 fusion.26
  130.5 6.7 fusion.5
  137.2 263.5 %all-gather.6.cloned.1.call-done = bf16[2048,4096]{1,0:T(8,128)(2,1)} async-done(((bf16[32,4096]{1,0:T(8,128)(2,1)}), bf16[2048,4096]{1,0:T(8,128)(2,1)}) %all-gather.6.cloned.1.call-update) | async-done | bytes 16777232 | tf_op jit(solution)/shard_map/all_gather | solution.py:55
  400.7 12.9 fusion.12
  413.6 4.2 multiply_reduce_fusion
  417.8 9.4 fusion.10
  427.3 57.8 %psum.21 = f32[4096]{0:T(1024)S(1)} all-reduce(f32[4096]{0:T(1024)S(1)} %fusion.10), channel_id=1, replica_groups=mesh['fsdp'=64,'seq'=4] {'seq'}, use_global_device_ids=true, to_apply=%region_6.7 | all-reduce | flops 4096 | bytes 32768 | tf_op jit(solution)/shard_map/psum | solution.py:59
  485.0 1.1 broadcast_multiply_fusion
  486.1 0.9 broadcast_multiply_fusion.1
  487.0 0.0 all-reduce.3.cloned.1.call-update
  487.1 0.0 reduce-scatter.3.cloned.1.call-start
  487.1 4.9 multiply_convert_fusion
  492.1 1.2 multiply_convert_fusion.1
  493.2 1.0 copy-done.4
  494.2 3.0 copy.48
  497.1 0.0 reduce-scatter.3.cloned.1.call-update
  497.2 0.3 reduce-scatter.5.cloned.1.call-start
  497.4 3.6 convolution_convert_fusion.1
  501.1 3.0 copy.50
  504.0 4.7 fusion.11
  508.8 0.5 copy.46
  509.3 1.2 convert_element_type.101
  510.5 645.8 %all-reduce.3.cloned.1.call-done = (f32[32,4096]{1,0:T(8,128)}, f32[64,4096]{1,0:T(8,128)}) async-done(((f32[32,4096]{1,0:T(8,128)}, f32[64,4096]{1,0:T(8,128)}), (f32[32,4096]{1,0:T(8,128)}, f32[64,4096]{1,0:T(8,128)})) %all-reduce.3.cloned.1.call-update) | async-done | bytes 1572880 | tf_op jit(solution)/shard_map/psum | solution.py:92
  1156.3 170.4 %reduce-scatter.3.cloned.1.call-done = bf16[192,2048]{1,0:T(8,128)(2,1)} async-done(((bf16[768,2048]{1,0:T(8,128)(2,1)}), bf16[192,2048]{1,0:T(8,128)(2,1)}) %reduce-scatter.3.cloned.1.call-update) | async-done | bytes 786448 | tf_op jit(solution)/shard_map/reduce_scatter | solution.py:81
  1326.7 69.1 %reduce-scatter.5.cloned.1.call-done = bf16[192,2048]{1,0:T(8,128)(2,1)} async-done(((bf16[768,2048]{1,0:T(8,128)(2,1)}), bf16[192,2048]{1,0:T(8,128)(2,1)}) %reduce-scatter.5.cloned.1.call-update) | async-done | bytes 786448 | tf_op jit(solution)/shard_map/reduce_scatter | solution.py:84
  1395.8 1.9 copy.78
  1397.7 2.3 copy.79
  (10 shorter events, 0.0 us)
Async XLA Ops:
  7.2 57.8 %all-gather.4.cloned.1.call-start = ((), (), s32[]{:S(2)}) async-start(), calls=%async_computation.2 | async-start | bytes 3932160 | tf_op jit(solution)/shard_map/all_gather | solution.py:36
  7.9 109.9 %all-gather.8.cloned.1.call-start = ((), (), s32[]{:S(2)}) async-start(), calls=%async_computation.4 | async-start | bytes 3932160 | tf_op jit(solution)/shard_map/all_gather | solution.py:37
  8.6 392.1 %all-gather.6.cloned.1.call-start = ((), (), s32[]{:S(2)}) async-start(), calls=%async_computation.3 | async-start | bytes 17039360 | tf_op jit(solution)/shard_map/all_gather | solution.py:55
  21.9 1134.4 %all-reduce.3.cloned.1.call-start = ((), (), s32[]{:S(2)}) async-start(), calls=%async_computation.7 | async-start | bytes 3145728 | tf_op jit(solution)/shard_map/psum | solution.py:92
  68.1 56.8 %copy-start = (bf16[1,768,2048]{1,2,0:T(8,128)(2,1)}, bf16[1,768,2048]{1,2,0:T(8,128)(2,1)S(1)}, u32[]{:S(2)}) copy-start(bf16[1,768,2048]{1,2,0:T(8,128)(2,1)S(1)} %copy.37) | copy-start | bytes 9437188
  400.7 12.9 copy-start.2
  413.6 4.2 copy-start.3
  487.1 839.6 %reduce-scatter.3.cloned.1.call-start = ((), (), s32[]{:S(2)}) async-start(), calls=%async_computation.5 | async-start | bytes 3932160 | tf_op jit(solution)/shard_map/reduce_scatter | solution.py:81
  487.1 5.0 copy-start.1
  492.1 2.1 copy-start.4
  497.2 898.7 %reduce-scatter.5.cloned.1.call-start = ((), (), s32[]{:S(2)}) async-start(), calls=%async_computation.6 | async-start | bytes 3932160 | tf_op jit(solution)/shard_map/reduce_scatter | solution.py:84
Sparse Core Ops, SparseCore 0:
  9.8 55.0 all-gather.3
  66.8 50.9 all-gather.7
  119.6 281.0 all-gather.5
  487.2 669.0 all-reduce.2
  1159.8 166.9 reduce-scatter.2
  1329.9 65.8 reduce-scatter.4
where the time goes:
time: 1410 us
  waiting for transfers between devices  1230 us (87%)
  blocking collectives  71 us (5%)
  matrix products  43.5 us (3%)
  local copies, waits for them, and re-layouts  26.5 us (2%)
  between operations  18.2 us (1%)
  other arithmetic  17.1 us (1%)
    psum x1, waiting for transfers between devices, shards(): lax.psum((time_hot, speaker_hot), 'fsdp')  646 us
    all_gather x1, waiting for transfers between devices, shards(): lax.all_gather(lax.all_gather(out_weight, 'seq', axis=1, tiled=True), 'fs...  264 us
    reduce_scatter x1, waiting for transfers between devices, shards(): lax.psum_scatter(key_term.astype(jnp.bfloat16), 'seq', scatter_dimension=...  170 us
    reduce_scatter x1, waiting for transfers between devices, shards(): lax.psum_scatter(value_term.astype(jnp.bfloat16), 'seq', scatter_dimensio...  69.1 us
    psum x1, blocking collectives, shards(): lax.psum(jnp.sum(grad_out.astype(jnp.float32) * proj, axis=0), 'seq')  57.8 us
    all_gather x1, waiting for transfers between devices, shards(): lax.all_gather(values, 'seq', axis=1, tiled=True)  49.7 us
    all_gather x1, waiting for transfers between devices, shards(): lax.all_gather(keys, 'seq', axis=1, tiled=True)  30.1 us
  transfers between devices with their start and end apart: 6, of which 6 were waited for; matrix products, arithmetic and copies ran while one was open for 4% of the time, Pallas kernels for 0%

commit v1 on v0

v1 whole, which is shorter than its diff:
```python
import functools
import math

import jax
import jax.numpy as jnp
from jax import lax
from jax.experimental import pallas as pl
from jax.experimental.pallas import tpu as pltpu
from jax.sharding import PartitionSpec as P

HEAD_DIM = 128
LOCAL_HEADS = 8
HALF = 384
ROWS = 192
FEAT = 1024
D = 4096
TT = 32
SPK = 64
SCALE = HEAD_DIM ** (-0.5)
SCALE2 = SCALE / math.log(2.0)
MESH = pl.DeviceIdType.MESH
BF = jnp.bfloat16
F32 = jnp.float32

NT = (((1,), (1,)), ((), ()))
NN = (((1,), (0,)), ((), ()))
TN = (((0,), (0,)), ((), ()))


def dot(a, b, dims):
    return lax.dot_general(a, b, dims, preferred_element_type=F32)


def kernel(
    ts_ref, sp_ref, ln_ref,
    q_in, k_in, v_in, g_in, w_in, tg_in, sg_in,
    dq_out, dk_out, dv_out, tt_out, st_out,
    qb, kb, vb, db, gb, sb, wb, ob, dqv, dkv, dvv, dka, dva, stats,
    gp, gx, zb, gat, ttv, stv, tgv, sgv,
    loc, ps, pr, wzs, wzr, ws, wr, zs, zr, ds_s, ds_r, g1, gzs, gzr, gxs, gxr, ol, os, orc,
):
    fs = lax.axis_index("fsdp")
    sq = lax.axis_index("seq")
    x = lax.rem(fs, 4)
    y = lax.rem(lax.div(fs, 4), 4)
    zl = lax.div(fs, 16)
    zh = lax.div(sq, 2)
    c = lax.rem(sq, 2)
    z = zh * 4 + zl
    oc = 1 - c

    def dev(dz=0, dy=0, dx=0, fc=0):
        z2 = lax.rem(z + dz, 8)
        y2 = lax.rem(y + dy, 4)
        x2 = lax.rem(x + dx, 4)
        c2 = oc if fc else c
        return (lax.rem(z2, 4) * 16 + y2 * 4 + x2, lax.div(z2, 4) * 2 + c2)

    def remote(src, dst, ss, rs, to):
        return pltpu.make_async_remote_copy(
            src_ref=src, dst_ref=dst, send_sem=ss, recv_sem=rs, device_id=to, device_id_type=MESH
        )

    partner = dev(fc=1)
    anti = dev(dz=4)

    bar = pltpu.get_barrier_semaphore()
    peers = [partner]
    peers += [dev(dz=d) for d in range(1, 8)]
    peers += [dev(dx=d) for d in range(1, 4)]
    peers += [dev(dy=d) for d in range(1, 4)]
    for p in peers:
        pl.semaphore_signal(bar, inc=1, device_id=p, device_id_type=MESH)
    pl.semaphore_wait(bar, len(peers))

    my_rows = pl.ds(pl.multiple_of(c * ROWS, 64), ROWS)
    ot_rows = pl.ds(pl.multiple_of(oc * ROWS, 64), ROWS)
    my_cols = pl.ds(pl.multiple_of(c * FEAT, FEAT), FEAT)
    ot_cols = pl.ds(pl.multiple_of(oc * FEAT, FEAT), FEAT)

    ch = lax.div(zl, 2)
    wt = lax.rem(zl, 2)
    wrow = pl.ds(pl.multiple_of(wt * 512 + y * 128 + x * 32, 32), 32)
    wcol = pl.ds(pl.multiple_of(sq * 1024, 1024), 1024)
    w_own = pltpu.make_async_copy(w_in, wb.at[wrow, wcol], loc.at[4])
    w_pair = remote(w_in, wb.at[wrow, wcol], ps.at[4], pr.at[4], partner)
    pl.when(c == ch)(w_own.start)
    pl.when(c != ch)(w_pair.start)

    pair = []
    for n, (src, dst) in enumerate(((k_in, kb), (v_in, vb), (q_in, qb))):
        pair.append((
            pltpu.make_async_copy(src.at[:, my_cols], dst.at[my_rows, :], loc.at[n]),
            remote(src.at[:, ot_cols], dst.at[my_rows, :], ps.at[n], pr.at[n], partner),
            remote(src.at[:, ot_cols], dst.at[ot_rows, :], ps.at[n], pr.at[n], partner),
        ))
    pair.append((
        pltpu.make_async_copy(g_in, gb.at[my_rows, :], loc.at[3]),
        remote(g_in, gb.at[my_rows, :], ps.at[3], pr.at[3], partner),
        remote(g_in, gb.at[ot_rows, :], ps.at[3], pr.at[3], partner),
    ))
    for a, b, _ in pair:
        b.start()
        a.start()
    tg_copy = pltpu.make_async_copy(tg_in, tgv, loc.at[5])
    sg_copy = pltpu.make_async_copy(sg_in, sgv, loc.at[6])
    tg_copy.start()
    sg_copy.start()

    wz_src = wb.at[wrow, pl.ds(pl.multiple_of(zh * 2048, 2048), 2048)]
    wz_out = [remote(wz_src, wz_src, wzs.at[d], wzr.at[wt * 2 + zh], dev(dz=d)) for d in range(1, 8)]

    @pl.when(c == ch)
    def _():
        w_own.wait()
        remote(
            w_in, wb.at[wrow, pl.ds(pl.multiple_of((zh * 2 + oc) * 1024, 1024), 1024)],
            ps.at[4], pr.at[4], partner,
        ).wait_recv()
        for cp in wz_out:
            cp.start()

    def head(j):
        return pl.ds(pl.multiple_of(j * HEAD_DIM, HEAD_DIM), HEAD_DIM)

    own = pl.ds(0, HALF)
    other = pl.ds(HALF, HALF)

    def zcopy(n, j):
        buf = (kb, vb, qb, db)[n]
        return remote(
            buf.at[own, head(j)], buf.at[other, head(j)], zs.at[n, j], zr.at[n, j], anti
        )

    def pair_wait(n):
        a, _, r = pair[n]
        a.wait()
        r.wait_recv()

    pair_wait(0)
    pair_wait(1)

    @pl.loop(0, LOCAL_HEADS)
    def _(j):
        zcopy(0, j).start()
        zcopy(1, j).start()

    pair_wait(2)

    @pl.loop(0, LOCAL_HEADS)
    def _(j):
        zcopy(2, j).start()

    tg_copy.wait()
    sg_copy.wait()
    gate = tgv[pl.ds(ts_ref[fs], 1), :] + sgv[pl.ds(sp_ref[fs], 1), :]
    pair_wait(3)
    for blk in range(8):
        cols = slice(blk * 512, (blk + 1) * 512)
        sb[:, cols] = (gb[:, cols].astype(F32) * gate[:, cols]).astype(BF)

    for t in range(2):
        for h in range(2):
            reg = wb.at[
                pl.ds(pl.multiple_of(t * 512 + y * 128 + x * 32, 32), 32),
                pl.ds(h * 2048, 2048),
            ]
            mine = jnp.logical_and(c == ch, jnp.logical_and(wt == t, zh == h))
            cp = remote(reg, reg, wzs.at[1], wzr.at[t * 2 + h], partner)
            pl.when(jnp.logical_not(mine))(cp.wait_recv)

    def unit(t, d1):
        if t == 0:
            r = y * 128 + lax.rem(x + 4 - d1, 4) * 32
        else:
            r = 512 + lax.rem(y + 4 - d1, 4) * 128 + x * 32
        return wb.at[pl.ds(pl.multiple_of(r, 32), 32), :]

    def axis_dev(axis, d):
        return dev(dx=d) if axis == 0 else dev(dy=d)

    def w1(t, d):
        return remote(unit(t, 0), unit(t, 0), ws.at[t, d, 0], wr.at[t, d, 0], axis_dev(t, d))

    def w2(t, d1, e):
        u = unit(t, d1)
        return remote(u, u, ws.at[t, d1, e], wr.at[t, d1, e], axis_dev(1 - t, e))

    for d in (1, 3, 2):
        for t in range(2):
            w1(t, d).start()
    for e in (1, 3, 2):
        for t in range(2):
            w2(t, 0, e).start()

    def w_forward():
        for d1 in (1, 3, 2):
            for t in range(2):
                u = unit(t, d1)
                remote(u, u, ws.at[t, d1, 0], wr.at[t, d1, 0], partner).wait_recv()
                for e in (1, 3, 2):
                    w2(t, d1, e).start()

    def w_finish():
        for d1 in range(4):
            for t in range(2):
                for e in range(1, 4):
                    if t == 0:
                        r = lax.rem(y + 4 - e, 4) * 128 + lax.rem(x + 4 - d1, 4) * 32
                    else:
                        r = 512 + lax.rem(y + 4 - d1, 4) * 128 + lax.rem(x + 4 - e, 4) * 32
                    u = wb.at[pl.ds(pl.multiple_of(r, 32), 32), :]
                    remote(u, u, ws.at[t, d1, e], wr.at[t, d1, e], partner).wait_recv()

    length = ln_ref[fs]
    key_pos = lax.broadcasted_iota(jnp.int32, (2 * HALF, 1), 0)
    frame = jnp.where(key_pos < HALF, zh * HALF + key_pos, (1 - zh) * HALF + key_pos - HALF)
    live = frame < length

    @pl.loop(0, LOCAL_HEADS)
    def _(j):
        pl.when(j == 1)(w_forward)
        zcopy(0, j).wait_recv()
        zcopy(1, j).wait_recv()
        s = dot(kb[:, head(j)], qb[own, head(j)], NT) * SCALE2
        s = jnp.where(live, s, -1e30)
        top = jnp.max(s, axis=0, keepdims=True)
        e = jnp.exp2(s - top)
        tot = jnp.sum(e, axis=0, keepdims=True)
        p = (e * (1.0 / tot)).astype(BF)
        ob[:, head(j)] = dot(p, vb[:, head(j)], TN).astype(BF)
        stats[0, j, 0:1, :] = top + jnp.log2(tot)

    w_finish()
    ones = jnp.ones((8, HEAD_DIM), F32)

    @pl.loop(0, LOCAL_HEADS // 2)
    def _(i):
        two = pl.ds(pl.multiple_of(i * 256, 256), 256)
        db[own, two] = dot(sb[...], wb[two, :], NT).astype(BF)
        for k in range(2):
            j = 2 * i + k
            prod = db[own, head(j)].astype(F32) * ob[:, head(j)].astype(F32)
            delta = lax.dot_general(
                ones, prod, NT, preferred_element_type=F32, precision=lax.Precision.HIGHEST
            )
            stats[0, j, 1:2, :] = delta[0:1, :]
            zcopy(3, j).start()
            remote(stats.at[0, j], stats.at[1, j], ds_s.at[j], ds_r.at[j], anti).start()

    @pl.loop(0, 16)
    def _(i):
        cols = pl.ds(pl.multiple_of(i * 256, 256), 256)
        proj = dot(ob[...], wb[:, cols], NN)
        part = jnp.sum(proj * gb[:, cols].astype(F32), axis=0, keepdims=True)
        gp[lax.div(i, 8), pl.ds(lax.rem(i, 8), 1), :] = part

    g1_copy = remote(gp.at[oc], gx, g1.at[0], g1.at[1], partner)
    g1_copy.start()

    gz_out = [remote(zb.at[z], zb.at[z], gzs.at[d], gzr.at[z], dev(dz=d)) for d in range(1, 8)]
    gx_src = gat.at[:, y, x]
    gx_out = [remote(gx_src, gx_src, gxs.at[0, d], gxr.at[0, d], dev(dx=d)) for d in range(1, 4)]
    gy_src = gat.at[:, y]
    gy_out = [remote(gy_src, gy_src, gxs.at[1, d], gxr.at[1, d], dev(dy=d)) for d in range(1, 4)]

    def gate_z():
        g1_copy.wait()
        zb[z] = gp[c] + gx[...]
        for cp in gz_out:
            cp.start()

    def gate_x():
        for d in range(1, 8):
            zz = lax.rem(z + d, 8)
            remote(zb.at[zz], zb.at[zz], gzs.at[d], gzr.at[zz], partner).wait_recv()
        for k in range(4):
            gat[k, y, x] = zb[k] + zb[k + 4]
        for cp in gx_out:
            cp.start()

    def gate_y():
        for d in range(1, 4):
            r = gat.at[:, y, lax.rem(x + 4 - d, 4)]
            remote(r, r, gxs.at[0, d], gxr.at[0, d], partner).wait_recv()
        for cp in gy_out:
            cp.start()

    my_tab = pl.ds(pl.multiple_of(c * 2048, 2048), 2048)
    tab = []
    for n, (src, dst) in enumerate(((ttv, tt_out), (stv, st_out))):
        tab.append(pltpu.make_async_copy(src, dst.at[:, my_tab], ol.at[3 + n]))
        tab.append(remote(src, dst.at[:, my_tab], os.at[3 + n], orc.at[3 + n], partner))

    def gate_tables():
        for d in range(1, 4):
            r = gat.at[:, lax.rem(y + 4 - d, 4)]
            remote(r, r, gxs.at[1, d], gxr.at[1, d], partner).wait_recv()
        tcol = jnp.concatenate([jnp.full((1, 1), ts_ref[k], jnp.int32) for k in range(64)], axis=1)
        scol = jnp.concatenate([jnp.full((1, 1), sp_ref[k], jnp.int32) for k in range(64)], axis=1)
        hot_t = (lax.broadcasted_iota(jnp.int32, (TT, 64), 0) == tcol).astype(F32)
        hot_s = (lax.broadcasted_iota(jnp.int32, (SPK, 64), 0) == scol).astype(F32)
        for r in range(8):
            rows = gat[:, :, :, r, :].reshape(64, 256)
            cols = slice(r * 256, (r + 1) * 256)
            for hot, dst in ((hot_t, ttv), (hot_s, stv)):
                dst[:, cols] = lax.dot_general(
                    hot, rows, NN, preferred_element_type=F32, precision=lax.Precision.HIGHEST
                )
        for cp in tab:
            cp.start()

    outs = ((dqv, dq_out), (dkv, dk_out), (dvv, dv_out))

    def out_copies(n, j):
        src, dst = outs[n]
        to = dst.at[:, pl.ds(pl.multiple_of(c * FEAT + j * HEAD_DIM, HEAD_DIM), HEAD_DIM)]
        return (
            pltpu.make_async_copy(src.at[my_rows, head(j)], to, ol.at[n]),
            remote(src.at[ot_rows, head(j)], to, os.at[n], orc.at[n], partner),
        )

    @pl.loop(0, LOCAL_HEADS)
    def _(j):
        q = qb[own, head(j)]
        k = kb[:, head(j)]
        do = db[own, head(j)]
        s = jnp.where(live, dot(k, q, NT) * SCALE2, -1e30)
        p = jnp.exp2(s - stats[0, j, 0:1, :])
        dp = dot(vb[:, head(j)], do, NT)
        ds = (p * (dp - stats[0, j, 1:2, :])).astype(BF)
        dqv[:, head(j)] = (dot(ds, k, TN) * SCALE).astype(BF)
        dka[:, head(j)] = dot(ds[:HALF], q, NN)
        dva[:, head(j)] = dot(p[:HALF].astype(BF), do, NN)
        for cp in out_copies(0, j):
            cp.start()
        pl.when(j == 0)(gate_z)
        pl.when(j == 3)(gate_x)
        pl.when(j == 5)(gate_y)

    gate_tables()

    @pl.loop(0, LOCAL_HEADS)
    def _(j):
        zcopy(2, j).wait_recv()
        zcopy(3, j).wait_recv()
        remote(stats.at[0, j], stats.at[1, j], ds_s.at[j], ds_r.at[j], anti).wait_recv()
        q = qb[other, head(j)]
        do = db[other, head(j)]
        s = jnp.where(live[:HALF], dot(kb[own, head(j)], q, NT) * SCALE2, -1e30)
        p = jnp.exp2(s - stats[1, j, 0:1, :])
        dp = dot(vb[own, head(j)], do, NT)
        ds = (p * (dp - stats[1, j, 1:2, :])).astype(BF)
        dkv[:, head(j)] = ((dka[:, head(j)] + dot(ds, q, NN)) * SCALE).astype(BF)
        dvv[:, head(j)] = (dva[:, head(j)] + dot(p.astype(BF), do, NN)).astype(BF)
        for n in (1, 2):
            for cp in out_copies(n, j):
                cp.start()

    for _, b, _ in pair:
        b.wait_send()
    pl.when(c != ch)(w_pair.wait_send)

    @pl.when(c == ch)
    def _():
        for cp in wz_out:
            cp.wait_send()

    for t in range(2):
        for d in range(1, 4):
            w1(t, d).wait_send()
        for d1 in range(4):
            for e in range(1, 4):
                w2(t, d1, e).wait_send()

    @pl.loop(0, LOCAL_HEADS)
    def _(j):
        for n in range(4):
            zcopy(n, j).wait_send()
        remote(stats.at[0, j], stats.at[1, j], ds_s.at[j], ds_r.at[j], anti).wait_send()

    for cp in gz_out + gx_out + gy_out:
        cp.wait_send()
    for n, (src, dst) in enumerate(outs):
        pltpu.make_async_copy(src.at[my_rows, :], dst.at[:, my_cols], ol.at[n]).wait()
        whole = remote(src.at[ot_rows, :], dst.at[:, ot_cols], os.at[n], orc.at[n], partner)
        whole.wait_send()
        whole.wait_recv()
    for cp in tab:
        cp.wait()


def shards(
    queries, keys, values, out_grad, out_weight, time_gate, speaker_gate, time_steps, speakers, lengths
):
    any_spec = pl.BlockSpec(memory_space=pl.ANY)
    smem = pl.BlockSpec(memory_space=pltpu.SMEM)
    dma = pltpu.SemaphoreType.DMA
    vm = pltpu.VMEM
    out_rows = jax.ShapeDtypeStruct((ROWS, 2 * FEAT), BF)
    dq, dk, dv, tt, st = pl.pallas_call(
        kernel,
        name="attention_grads",
        out_shape=(
            out_rows, out_rows, out_rows,
            jax.ShapeDtypeStruct((TT, D), F32), jax.ShapeDtypeStruct((SPK, D), F32),
        ),
        in_specs=[smem] * 3 + [any_spec] * 7,
        out_specs=(any_spec,) * 5,
        scratch_shapes=[
            vm((2 * HALF, FEAT), BF), vm((2 * HALF, FEAT), BF), vm((2 * HALF, FEAT), BF),
            vm((2 * HALF, FEAT), BF),
            vm((HALF, D), BF), vm((HALF, D), BF), vm((FEAT, D), BF), vm((HALF, FEAT), BF),
            vm((HALF, FEAT), BF), vm((HALF, FEAT), BF), vm((HALF, FEAT), BF),
            vm((HALF, FEAT), F32), vm((HALF, FEAT), F32),
            vm((2, LOCAL_HEADS, 8, HALF), F32),
            vm((2, 8, 256), F32), vm((8, 256), F32), vm((8, 8, 256), F32),
            vm((4, 4, 4, 8, 256), F32),
            vm((TT, 2048), F32), vm((SPK, 2048), F32), vm((TT, D), F32), vm((SPK, D), F32),
            dma((8,)), dma((5,)), dma((5,)), dma((8,)), dma((4,)),
            dma((2, 4, 4)), dma((2, 4, 4)), dma((4, 8)), dma((4, 8)), dma((8,)), dma((8,)),
            dma((2,)), dma((8,)), dma((8,)), dma((2, 4)), dma((2, 4)),
            dma((5,)), dma((5,)), dma((5,)),
        ],
        compiler_params=pltpu.CompilerParams(
            collective_id=0, has_side_effects=True, vmem_limit_bytes=58 * 2**20
        ),
    )(
        time_steps, speakers, lengths,
        queries[0], keys[0], values[0], out_grad[0], out_weight, time_gate, speaker_gate,
    )
    return dq[None], dk[None], dv[None], tt, st


def solution(mesh):
    rows = P("fsdp", "seq", None)
    in_specs = (rows, rows, rows, rows, P("fsdp", "seq"), P(), P(), P(), P(), P())
    out_specs = (rows, rows, rows, P(), P())
    return jax.shard_map(shards, mesh=mesh, in_specs=in_specs, out_specs=out_specs, check_vma=False)
```

time: 1410 us -> 227 us (0.16)
  waiting for transfers between devices: 1230 us -> 0 us
  Pallas kernels: 0 us -> 218 us
  blocking collectives: 71 us -> 0 us
  matrix products: 43.5 us -> 0 us
  local copies, waits for them, and re-layouts: 26.5 us -> 5.74 us
  between operations: 18.2 us -> 0.66 us
  other arithmetic: 17.1 us -> 0 us
    psum x1 -> x0, waiting for transfers between devices: 646 us -> none  [shards(): lax.psum((time_hot, speaker_hot), 'fsdp')]
    all_gather x3 -> x0, waiting for transfers between devices: 343 us -> none  [the longest x1 264 us: shards(): lax.all_gather(lax.all_gather(out_weight, 'seq', axis=1, tiled=True), 'fs...]
    reduce_scatter x2 -> x0, waiting for transfers between devices: 240 us -> none  [the longest x1 170 us: shards(): lax.psum_scatter(key_term.astype(jnp.bfloat16), 'seq', scatter_dimension=...]
    pallas_call x0 -> x1, Pallas kernels: none -> 218 us  [shards(): pl.pallas_call(kernel, name='attention_grads', out_shape=(out_rows, out_r...]
    psum x1 -> x0, blocking collectives: 57.8 us -> none  [shards(): lax.psum(jnp.sum(grad_out.astype(jnp.float32) * proj, axis=0), 'seq')]
    dot_general x8 -> x0, matrix products: 43.5 us -> none  [the longest x1 12.9 us: shards(): lax.dot_general(scaled, weight_full, (((1,), (1,)), ((), ())), preferred_...]
  transfers between devices with their start and end apart: 6 -> 0, of which waited for: 6 -> 0; matrix products, arithmetic and copies ran while one was open for 4% -> 0% of each run, Pallas kernels for 0% -> 0%
where the time goes in v1:
time: 227 us; the launch traced here: 224 us
  Pallas kernels  218 us (96%)
  local copies, waits for them, and re-layouts  5.74 us (3%)
    pallas_call x1, Pallas kernels, shards(): pl.pallas_call(kernel, name='attention_grads', out_shape=(out_rows, out_r...  218 us
    unnamed x13, local copies, waits for them, and re-layouts  5.74 us

profile of v1, /device:TPU:71, one launch (start us, length us, event | category | flops | bytes accessed | tf_op | source)
XLA Modules:
  0.0 224.0 jit_solution(3137508931590066584)
XLA Ops:
  0.6 217.6 %attention_grads.1 = (bf16[192,2048]{1,0:T(8,128)(2,1)}, bf16[192,2048]{1,0:T(8,128)(2,1)}, bf16[192,2048]{1,0:T(8,128)(2,1)}, f32[32,4096]{1,0:T(8,128)}, f32[64,4096]{1,0:T(8,128)}) custom-call(s32[64]{0:T(128)} %ts_ref.1, s32[64]{0:T(128)} %sp_ref.1, s32[64]{0:T(128)} %ln_ref.1, bf16[192,2048]{1,0:T(8,128)(2,1)} %bitcast.8, bf16[192,2048]{1,0:T(8,128)(2,1)} %bitcast.9, ...), custom_call_target="tpu_custom_call" | custom-call | tf_op jit(solution)/shard_map/attention_grads/pallas_call | solution.py:401
  218.3 0.0 copy-start.2
  218.3 0.0 copy-start.1
  218.3 2.2 copy.20
  220.5 0.0 copy-done.2
  220.5 0.0 copy-start.3
  220.5 0.9 copy.21
  221.4 0.0 copy-done.1
  221.4 0.0 copy-start
  221.4 0.9 copy.22
  222.3 0.0 copy-done.3
  222.3 0.8 copy.23
  223.1 0.0 copy-done
  223.1 1.0 copy.24
Async XLA Ops:
  218.3 2.2 copy-start.2
  218.3 3.1 %copy-start.1 = (bf16[192,2048]{1,0:T(8,128)(2,1)S(1)}, bf16[192,2048]{1,0:T(8,128)(2,1)}, u32[]{:S(2)}) copy-start(bf16[192,2048]{1,0:T(8,128)(2,1)} %get-tuple-element.12) | copy-start | bytes 2359300
  220.5 1.8 copy-start.3
  221.4 1.7 copy-start

commit v2 on v1

--- a/solution.py
+++ b/solution.py
@@ -107,8 +107,35 @@
     tg_copy.start()
     sg_copy.start()
 
-    wz_src = wb.at[wrow, pl.ds(pl.multiple_of(zh * 2048, 2048), 2048)]
-    wz_out = [remote(wz_src, wz_src, wzs.at[d], wzr.at[wt * 2 + zh], dev(dz=d)) for d in range(1, 8)]
+    def head(j):
+        return pl.ds(pl.multiple_of(j * HEAD_DIM, HEAD_DIM), HEAD_DIM)
+
+    own = pl.ds(0, HALF)
+    other = pl.ds(HALF, HALF)
+
+    def zcopy(n, j):
+        buf = (kb, vb, qb, db)[n]
+        return remote(
+            buf.at[own, head(j)], buf.at[other, head(j)], zs.at[n, j], zr.at[n, j], anti
+        )
+
+    def pair_wait(n):
+        a, _, r = pair[n]
+        a.wait()
+        r.wait_recv()
+
+    def wblock(t, h):
+        return wb.at[
+            pl.ds(pl.multiple_of(t * 512 + y * 128 + x * 32, 32), 32), pl.ds(h * 2048, 2048)
+        ]
+
+    wblocks = []
+    for t in range(2):
+        for h in range(2):
+            wblocks.append((t, h, lax.rem(z + 16 - (4 * h + 2 * c + t), 8)))
+
+    def wz(t, h, n, d):
+        return remote(wblock(t, h), wblock(t, h), wzs.at[t * 2 + h, n], wzr.at[t * 2 + h], dev(dz=d))
 
     @pl.when(c == ch)
     def _():
@@ -117,57 +144,44 @@
             w_in, wb.at[wrow, pl.ds(pl.multiple_of((zh * 2 + oc) * 1024, 1024), 1024)],
             ps.at[4], pr.at[4], partner,
         ).wait_recv()
-        for cp in wz_out:
-            cp.start()
-
-    def head(j):
-        return pl.ds(pl.multiple_of(j * HEAD_DIM, HEAD_DIM), HEAD_DIM)
-
-    own = pl.ds(0, HALF)
-    other = pl.ds(HALF, HALF)
-
-    def zcopy(n, j):
-        buf = (kb, vb, qb, db)[n]
-        return remote(
-            buf.at[own, head(j)], buf.at[other, head(j)], zs.at[n, j], zr.at[n, j], anti
-        )
-
-    def pair_wait(n):
-        a, _, r = pair[n]
-        a.wait()
-        r.wait_recv()
+
+    def wz_start(t, h, hops):
+        def go():
+            for n, d in enumerate(hops):
+                wz(t, h, n, d).start()
+        return go
+
+    def wz_sent(t, h, hops):
+        def go():
+            for n, d in enumerate(hops):
+                wz(t, h, n, d).wait_send()
+        return go
+
+    def wz_pass(t, h, hops):
+        def go():
+            wz(t, h, 0, 1).wait_recv()
+            wz_start(t, h, hops)()
+        return go
+
+    W0, W2, W6 = (2, 6), (1, 7, 2), (1, 7)
+    for t, h, d in wblocks:
+        pl.when(d == 0)(wz_start(t, h, W0))
 
     pair_wait(0)
     pair_wait(1)
-
-    @pl.loop(0, LOCAL_HEADS)
-    def _(j):
-        zcopy(0, j).start()
-        zcopy(1, j).start()
-
-    pair_wait(2)
-
-    @pl.loop(0, LOCAL_HEADS)
-    def _(j):
-        zcopy(2, j).start()
-
-    tg_copy.wait()
-    sg_copy.wait()
-    gate = tgv[pl.ds(ts_ref[fs], 1), :] + sgv[pl.ds(sp_ref[fs], 1), :]
-    pair_wait(3)
-    for blk in range(8):
-        cols = slice(blk * 512, (blk + 1) * 512)
-        sb[:, cols] = (gb[:, cols].astype(F32) * gate[:, cols]).astype(BF)
-
-    for t in range(2):
-        for h in range(2):
-            reg = wb.at[
-                pl.ds(pl.multiple_of(t * 512 + y * 128 + x * 32, 32), 32),
-                pl.ds(h * 2048, 2048),
-            ]
-            mine = jnp.logical_and(c == ch, jnp.logical_and(wt == t, zh == h))
-            cp = remote(reg, reg, wzs.at[1], wzr.at[t * 2 + h], partner)
-            pl.when(jnp.logical_not(mine))(cp.wait_recv)
+    zcopy(0, 0).start()
+    zcopy(1, 0).start()
+
+    for t, h, d in wblocks:
+        pl.when(d == 2)(wz_pass(t, h, W2))
+        pl.when(d == 6)(wz_pass(t, h, W6))
+
+    zcopy(0, 1).start()
+    zcopy(1, 1).start()
+
+    for t, h, d in wblocks:
+        last = jnp.logical_or(lax.rem(d, 2) == 1, d == 4)
+        pl.when(last)(wz(t, h, 0, 1).wait_recv)
 
     def unit(t, d1):
         if t == 0:
@@ -212,6 +226,25 @@
                     u = wb.at[pl.ds(pl.multiple_of(r, 32), 32), :]
                     remote(u, u, ws.at[t, d1, e], wr.at[t, d1, e], partner).wait_recv()
 
+    @pl.loop(2, LOCAL_HEADS)
+    def _(j):
+        zcopy(0, j).start()
+        zcopy(1, j).start()
+
+    pair_wait(2)
+
+    @pl.loop(0, LOCAL_HEADS)
+    def _(j):
+        zcopy(2, j).start()
+
+    tg_copy.wait()
+    sg_copy.wait()
+    gate = tgv[pl.ds(ts_ref[fs], 1), :] + sgv[pl.ds(sp_ref[fs], 1), :]
+    pair_wait(3)
+    for blk in range(8):
+        cols = slice(blk * 512, (blk + 1) * 512)
+        sb[:, cols] = (gb[:, cols].astype(F32) * gate[:, cols]).astype(BF)
+
     length = ln_ref[fs]
     key_pos = lax.broadcasted_iota(jnp.int32, (2 * HALF, 1), 0)
     frame = jnp.where(key_pos < HALF, zh * HALF + key_pos, (1 - zh) * HALF + key_pos - HALF)
@@ -229,24 +262,9 @@
         tot = jnp.sum(e, axis=0, keepdims=True)
         p = (e * (1.0 / tot)).astype(BF)
         ob[:, head(j)] = dot(p, vb[:, head(j)], TN).astype(BF)
-        stats[0, j, 0:1, :] = top + jnp.log2(tot)
+        stats[0, 0, pl.ds(j, 1), :] = top + jnp.log2(tot)
 
     w_finish()
-    ones = jnp.ones((8, HEAD_DIM), F32)
-
-    @pl.loop(0, LOCAL_HEADS // 2)
-    def _(i):
-        two = pl.ds(pl.multiple_of(i * 256, 256), 256)
-        db[own, two] = dot(sb[...], wb[two, :], NT).astype(BF)
-        for k in range(2):
-            j = 2 * i + k
-            prod = db[own, head(j)].astype(F32) * ob[:, head(j)].astype(F32)
-            delta = lax.dot_general(
-                ones, prod, NT, preferred_element_type=F32, precision=lax.Precision.HIGHEST
-            )
-            stats[0, j, 1:2, :] = delta[0:1, :]
-            zcopy(3, j).start()
-            remote(stats.at[0, j], stats.at[1, j], ds_s.at[j], ds_r.at[j], anti).start()
 
     @pl.loop(0, 16)
     def _(i):
@@ -310,6 +328,28 @@
         for cp in tab:
             cp.start()
 
+    gate_z()
+    ones = jnp.ones((8, HEAD_DIM), F32)
+
+    @pl.loop(0, LOCAL_HEADS // 2)
+    def _(i):
+        two = pl.ds(pl.multiple_of(i * 256, 256), 256)
+        db[own, two] = dot(sb[...], wb[two, :], NT).astype(BF)
+        for k in range(2):
+            j = 2 * i + k
+            prod = db[own, head(j)].astype(F32) * ob[:, head(j)].astype(F32)
+            delta = lax.dot_general(
+                ones, prod, NT, preferred_element_type=F32, precision=lax.Precision.HIGHEST
+            )
+            stats[0, 1, pl.ds(j, 1), :] = delta[0:1, :]
+
+    stat_copy = remote(stats.at[0], stats.at[1], ds_s.at[0], ds_r.at[0], anti)
+    stat_copy.start()
+
+    @pl.loop(0, LOCAL_HEADS)
+    def _(j):
+        zcopy(3, j).start()
+
     outs = ((dqv, dq_out), (dkv, dk_out), (dvv, dv_out))
 
     def out_copies(n, j):
@@ -326,31 +366,30 @@
         k = kb[:, head(j)]
         do = db[own, head(j)]
         s = jnp.where(live, dot(k, q, NT) * SCALE2, -1e30)
-        p = jnp.exp2(s - stats[0, j, 0:1, :])
+        p = jnp.exp2(s - stats[0, 0, pl.ds(j, 1), :])
         dp = dot(vb[:, head(j)], do, NT)
-        ds = (p * (dp - stats[0, j, 1:2, :])).astype(BF)
+        ds = (p * (dp - stats[0, 1, pl.ds(j, 1), :])).astype(BF)
         dqv[:, head(j)] = (dot(ds, k, TN) * SCALE).astype(BF)
         dka[:, head(j)] = dot(ds[:HALF], q, NN)
         dva[:, head(j)] = dot(p[:HALF].astype(BF), do, NN)
         for cp in out_copies(0, j):
             cp.start()
-        pl.when(j == 0)(gate_z)
-        pl.when(j == 3)(gate_x)
-        pl.when(j == 5)(gate_y)
-
-    gate_tables()
-
-    @pl.loop(0, LOCAL_HEADS)
-    def _(j):
+
+    gate_x()
+    stat_copy.wait_recv()
+
+    @pl.loop(0, LOCAL_HEADS)
+    def _(j):
+        pl.when(j == 1)(gate_y)
+        pl.when(j == 3)(gate_tables)
         zcopy(2, j).wait_recv()
         zcopy(3, j).wait_recv()
-        remote(stats.at[0, j], stats.at[1, j], ds_s.at[j], ds_r.at[j], anti).wait_recv()
         q = qb[other, head(j)]
         do = db[other, head(j)]
         s = jnp.where(live[:HALF], dot(kb[own, head(j)], q, NT) * SCALE2, -1e30)
-        p = jnp.exp2(s - stats[1, j, 0:1, :])
+        p = jnp.exp2(s - stats[1, 0, pl.ds(j, 1), :])
         dp = dot(vb[own, head(j)], do, NT)
-        ds = (p * (dp - stats[1, j, 1:2, :])).astype(BF)
+        ds = (p * (dp - stats[1, 1, pl.ds(j, 1), :])).astype(BF)
         dkv[:, head(j)] = ((dka[:, head(j)] + dot(ds, q, NN)) * SCALE).astype(BF)
         dvv[:, head(j)] = (dva[:, head(j)] + dot(p.astype(BF), do, NN)).astype(BF)
         for n in (1, 2):
@@ -361,10 +400,10 @@
         b.wait_send()
     pl.when(c != ch)(w_pair.wait_send)
 
-    @pl.when(c == ch)
-    def _():
-        for cp in wz_out:
-            cp.wait_send()
+    for t, h, d in wblocks:
+        pl.when(d == 0)(wz_sent(t, h, W0))
+        pl.when(d == 2)(wz_sent(t, h, W2))
+        pl.when(d == 6)(wz_sent(t, h, W6))
 
     for t in range(2):
         for d in range(1, 4):
@@ -377,9 +416,8 @@
     def _(j):
         for n in range(4):
             zcopy(n, j).wait_send()
-        remote(stats.at[0, j], stats.at[1, j], ds_s.at[j], ds_r.at[j], anti).wait_send()
-
-    for cp in gz_out + gx_out + gy_out:
+
+    for cp in [stat_copy] + gz_out + gx_out + gy_out:
         cp.wait_send()
     for n, (src, dst) in enumerate(outs):
         pltpu.make_async_copy(src.at[my_rows, :], dst.at[:, my_cols], ol.at[n]).wait()
@@ -413,12 +451,12 @@
             vm((HALF, D), BF), vm((HALF, D), BF), vm((FEAT, D), BF), vm((HALF, FEAT), BF),
             vm((HALF, FEAT), BF), vm((HALF, FEAT), BF), vm((HALF, FEAT), BF),
             vm((HALF, FEAT), F32), vm((HALF, FEAT), F32),
-            vm((2, LOCAL_HEADS, 8, HALF), F32),
+            vm((2, 2, LOCAL_HEADS, HALF), F32),
             vm((2, 8, 256), F32), vm((8, 256), F32), vm((8, 8, 256), F32),
             vm((4, 4, 4, 8, 256), F32),
             vm((TT, 2048), F32), vm((SPK, 2048), F32), vm((TT, D), F32), vm((SPK, D), F32),
-            dma((8,)), dma((5,)), dma((5,)), dma((8,)), dma((4,)),
-            dma((2, 4, 4)), dma((2, 4, 4)), dma((4, 8)), dma((4, 8)), dma((8,)), dma((8,)),
+            dma((8,)), dma((5,)), dma((5,)), dma((4, 3)), dma((4,)),
+            dma((2, 4, 4)), dma((2, 4, 4)), dma((4, 8)), dma((4, 8)), dma((1,)), dma((1,)),
             dma((2,)), dma((8,)), dma((8,)), dma((2, 4)), dma((2, 4)),
             dma((5,)), dma((5,)), dma((5,)),
         ],

time: 227 us -> 184 us (0.81); the launches traced: 224 us -> 184 us
  Pallas kernels: 218 us -> 177 us
    pallas_call x1, Pallas kernels: 218 us -> 177 us  [shards(): pl.pallas_call(kernel, name='attention_grads', out_shape=(out_rows, out_r...]
where the time goes in v2:
time: 184 us
  Pallas kernels  177 us (96%)
  local copies, waits for them, and re-layouts  5.74 us (3%)
    pallas_call x1, Pallas kernels, shards(): pl.pallas_call(kernel, name='attention_grads', out_shape=(out_rows, out_r...  177 us
    unnamed x13, local copies, waits for them, and re-layouts  5.74 us

profile of v2, /device:TPU:71, one launch (start us, length us, event | category | flops | bytes accessed | tf_op | source)
XLA Modules:
  0.0 183.6 jit_solution(2830239032551648168)
XLA Ops:
  0.6 177.2 %attention_grads.1 = (bf16[192,2048]{1,0:T(8,128)(2,1)}, bf16[192,2048]{1,0:T(8,128)(2,1)}, bf16[192,2048]{1,0:T(8,128)(2,1)}, f32[32,4096]{1,0:T(8,128)}, f32[64,4096]{1,0:T(8,128)}) custom-call(s32[64]{0:T(128)} %ts_ref.1, s32[64]{0:T(128)} %sp_ref.1, s32[64]{0:T(128)} %ln_ref.1, bf16[192,2048]{1,0:T(8,128)(2,1)} %bitcast.8, bf16[192,2048]{1,0:T(8,128)(2,1)} %bitcast.9, ...), custom_call_target="tpu_custom_call" | custom-call | tf_op jit(solution)/shard_map/attention_grads/pallas_call | solution.py:439
  177.8 0.0 copy-start.2
  177.8 0.0 copy-start.1
  177.8 2.2 %copy.20 = bf16[1,192,2048]{2,1,0:T(8,128)(2,1)} copy(bf16[1,192,2048]{2,1,0:T(8,128)(2,1)} %bitcast.13) | data formatting | bytes 1572864
  180.1 0.0 copy-done.2
  180.1 0.0 copy-start.3
  180.1 0.9 copy.21
  180.9 0.0 copy-done.1
  180.9 0.0 copy-start
  180.9 0.9 copy.22
  181.8 0.0 copy-done.3
  181.8 0.8 copy.23
  182.6 0.0 copy-done
  182.6 1.0 copy.24
Async XLA Ops:
  177.8 2.2 %copy-start.2 = (bf16[192,2048]{1,0:T(8,128)(2,1)S(1)}, bf16[192,2048]{1,0:T(8,128)(2,1)}, u32[]{:S(2)}) copy-start(bf16[192,2048]{1,0:T(8,128)(2,1)} %get-tuple-element.11) | copy-start | bytes 2359300
  177.8 3.1 %copy-start.1 = (bf16[192,2048]{1,0:T(8,128)(2,1)S(1)}, bf16[192,2048]{1,0:T(8,128)(2,1)}, u32[]{:S(2)}) copy-start(bf16[192,2048]{1,0:T(8,128)(2,1)} %get-tuple-element.12) | copy-start | bytes 2359300
  180.1 1.8 copy-start.3
  180.9 1.7 copy-start

commit v3 on v2

--- a/solution.py
+++ b/solution.py
@@ -37,7 +37,7 @@
     dq_out, dk_out, dv_out, tt_out, st_out,
     qb, kb, vb, db, gb, sb, wb, ob, dqv, dkv, dvv, dka, dva, stats,
     gp, gx, zb, gat, ttv, stv, tgv, sgv,
-    loc, ps, pr, wzs, wzr, ws, wr, zs, zr, ds_s, ds_r, g1, gzs, gzr, gxs, gxr, ol, os, orc,
+    loc, ps, pr, wzs, wzr, ws, wsr, wr, zs, zr, ds_s, ds_r, g1, gzs, gzr, gxs, gxr, ol, os, orc,
 ):
     fs = lax.axis_index("fsdp")
     sq = lax.axis_index("seq")
@@ -183,48 +183,81 @@
         last = jnp.logical_or(lax.rem(d, 2) == 1, d == 4)
         pl.when(last)(wz(t, h, 0, 1).wait_recv)
 
-    def unit(t, d1):
+    def unit(t, d, e, half=None):
         if t == 0:
-            r = y * 128 + lax.rem(x + 4 - d1, 4) * 32
+            r = lax.rem(y + 4 - e, 4) * 128 + lax.rem(x + 4 - d, 4) * 32
         else:
-            r = 512 + lax.rem(y + 4 - d1, 4) * 128 + x * 32
+            r = 512 + lax.rem(y + 4 - d, 4) * 128 + lax.rem(x + 4 - e, 4) * 32
+        if half is not None:
+            return wb.at[pl.ds(pl.multiple_of(r + 16 * half, 16), 16), :]
         return wb.at[pl.ds(pl.multiple_of(r, 32), 32), :]
 
     def axis_dev(axis, d):
         return dev(dx=d) if axis == 0 else dev(dy=d)
 
     def w1(t, d):
-        return remote(unit(t, 0), unit(t, 0), ws.at[t, d, 0], wr.at[t, d, 0], axis_dev(t, d))
-
-    def w2(t, d1, e):
-        u = unit(t, d1)
-        return remote(u, u, ws.at[t, d1, e], wr.at[t, d1, e], axis_dev(1 - t, e))
-
-    for d in (1, 3, 2):
+        u = unit(t, 0, 0)
+        return remote(u, u, ws.at[t, d, 0], wr.at[t, d, 0], axis_dev(t, d))
+
+    def w2(t, d, e):
+        u = unit(t, d, 0)
+        return remote(u, u, ws.at[t, d, e], wr.at[t, d, e], axis_dev(1 - t, e))
+
+    def w1_relay(t, d):
+        u = unit(t, d, 0, (d - 1) // 2)
+        return remote(u, u, wsr.at[t, 0, d], wr.at[t, 2, 0], axis_dev(t, d))
+
+    def w2_relay(t, d, e):
+        u = unit(t, d, e, (e - 1) // 2)
+        return remote(u, u, wsr.at[t, 1 + d, e], wr.at[t, d, 2], axis_dev(1 - t, e))
+
+    def w_wait(t, d, e):
+        u = unit(t, d, e)
+        remote(u, u, ws.at[t, d, e], wr.at[t, d, e], partner).wait_recv()
+
+    near = (1, 3)
+    for d in near:
         for t in range(2):
             w1(t, d).start()
-    for e in (1, 3, 2):
+    for e in near:
         for t in range(2):
             w2(t, 0, e).start()
 
-    def w_forward():
-        for d1 in (1, 3, 2):
+    def w_stage0():
+        for d in near:
             for t in range(2):
-                u = unit(t, d1)
-                remote(u, u, ws.at[t, d1, 0], wr.at[t, d1, 0], partner).wait_recv()
-                for e in (1, 3, 2):
-                    w2(t, d1, e).start()
+                w_wait(t, d, 0)
+                w1_relay(t, d).start()
+                for e in near:
+                    w2(t, d, e).start()
+
+    def w_stage1():
+        for e in near:
+            for t in range(2):
+                w_wait(t, 0, e)
+                w2_relay(t, 0, e).start()
+        for t in range(2):
+            w_wait(t, 2, 0)
+            for e in near:
+                w2(t, 2, e).start()
+
+    def w_stage2():
+        for d in near:
+            for e in near:
+                for t in range(2):
+                    w_wait(t, d, e)
+                    w2_relay(t, d, e).start()
+
+    def w_stage3():
+        for e in near:
+            for t in range(2):
+                w_wait(t, 2, e)
+                w2_relay(t, 2, e).start()
 
     def w_finish():
-        for d1 in range(4):
+        for d in range(4):
             for t in range(2):
-                for e in range(1, 4):
-                    if t == 0:
-                        r = lax.rem(y + 4 - e, 4) * 128 + lax.rem(x + 4 - d1, 4) * 32
-                    else:
-                        r = 512 + lax.rem(y + 4 - d1, 4) * 128 + lax.rem(x + 4 - e, 4) * 32
-                    u = wb.at[pl.ds(pl.multiple_of(r, 32), 32), :]
-                    remote(u, u, ws.at[t, d1, e], wr.at[t, d1, e], partner).wait_recv()
+                w_wait(t, d, 2)
 
     @pl.loop(2, LOCAL_HEADS)
     def _(j):
@@ -252,7 +285,8 @@
 
     @pl.loop(0, LOCAL_HEADS)
     def _(j):
-        pl.when(j == 1)(w_forward)
+        for n, stage in enumerate((w_stage0, w_stage1, w_stage2, w_stage3)):
+            pl.when(j == n)(stage)
         zcopy(0, j).wait_recv()
         zcopy(1, j).wait_recv()
         s = dot(kb[:, head(j)], qb[own, head(j)], NT) * SCALE2
@@ -375,13 +409,13 @@
         for cp in out_copies(0, j):
             cp.start()
 
-    gate_x()
     stat_copy.wait_recv()
 
     @pl.loop(0, LOCAL_HEADS)
     def _(j):
-        pl.when(j == 1)(gate_y)
-        pl.when(j == 3)(gate_tables)
+        pl.when(j == 2)(gate_x)
+        pl.when(j == 4)(gate_y)
+        pl.when(j == 6)(gate_tables)
         zcopy(2, j).wait_recv()
         zcopy(3, j).wait_recv()
         q = qb[other, head(j)]
@@ -406,11 +440,13 @@
         pl.when(d == 6)(wz_sent(t, h, W6))
 
     for t in range(2):
-        for d in range(1, 4):
+        for d in near:
             w1(t, d).wait_send()
-        for d1 in range(4):
-            for e in range(1, 4):
-                w2(t, d1, e).wait_send()
+            w1_relay(t, d).wait_send()
+        for d in range(4):
+            for e in near:
+                w2(t, d, e).wait_send()
+                w2_relay(t, d, e).wait_send()
 
     @pl.loop(0, LOCAL_HEADS)
     def _(j):
@@ -456,7 +492,7 @@
             vm((4, 4, 4, 8, 256), F32),
             vm((TT, 2048), F32), vm((SPK, 2048), F32), vm((TT, D), F32), vm((SPK, D), F32),
             dma((8,)), dma((5,)), dma((5,)), dma((4, 3)), dma((4,)),
-            dma((2, 4, 4)), dma((2, 4, 4)), dma((4, 8)), dma((4, 8)), dma((1,)), dma((1,)),
+            dma((2, 4, 4)), dma((2, 5, 4)), dma((2, 4, 4)), dma((4, 8)), dma((4, 8)), dma((1,)), dma((1,)),
             dma((2,)), dma((8,)), dma((8,)), dma((2, 4)), dma((2, 4)),
             dma((5,)), dma((5,)), dma((5,)),
         ],

time: 184 us -> 182 us (0.989)
  Pallas kernels: 177 us -> 175 us
    pallas_call x1, Pallas kernels: 177 us -> 175 us  [shards(): pl.pallas_call(kernel, name='attention_grads', out_shape=(out_rows, out_r...]
where the time goes in v3:
time: 182 us; the launch traced here: 181 us
  Pallas kernels  175 us (96%)
  local copies, waits for them, and re-layouts  5.74 us (3%)
    pallas_call x1, Pallas kernels, shards(): pl.pallas_call(kernel, name='attention_grads', out_shape=(out_rows, out_r...  175 us
    unnamed x13, local copies, waits for them, and re-layouts  5.74 us

profile of v3, /device:TPU:71, one launch (start us, length us, event | category | flops | bytes accessed | tf_op | source)
XLA Modules:
  0.0 181.2 jit_solution(12886947528776593231)
XLA Ops:
  0.6 174.8 %attention_grads.1 = (bf16[192,2048]{1,0:T(8,128)(2,1)}, bf16[192,2048]{1,0:T(8,128)(2,1)}, bf16[192,2048]{1,0:T(8,128)(2,1)}, f32[32,4096]{1,0:T(8,128)}, f32[64,4096]{1,0:T(8,128)}) custom-call(s32[64]{0:T(128)} %ts_ref.1, s32[64]{0:T(128)} %sp_ref.1, s32[64]{0:T(128)} %ln_ref.1, bf16[192,2048]{1,0:T(8,128)(2,1)} %bitcast.8, bf16[192,2048]{1,0:T(8,128)(2,1)} %bitcast.9, ...), custom_call_target="tpu_custom_call" | custom-call | tf_op jit(solution)/shard_map/attention_grads/pallas_call | solution.py:475
  175.4 0.0 copy-start.2
  175.4 0.0 copy-start.1
  175.4 2.2 %copy.20 = bf16[1,192,2048]{2,1,0:T(8,128)(2,1)} copy(bf16[1,192,2048]{2,1,0:T(8,128)(2,1)} %bitcast.13) | data formatting | bytes 1572864
  177.6 0.0 copy-done.2
  177.6 0.0 copy-start.3
  177.6 0.9 copy.21
  178.5 0.0 copy-done.1
  178.5 0.0 copy-start
  178.5 0.9 copy.22
  179.4 0.0 copy-done.3
  179.4 0.8 copy.23
  180.2 0.0 copy-done
  180.2 1.0 copy.24
Async XLA Ops:
  175.4 2.2 %copy-start.2 = (bf16[192,2048]{1,0:T(8,128)(2,1)S(1)}, bf16[192,2048]{1,0:T(8,128)(2,1)}, u32[]{:S(2)}) copy-start(bf16[192,2048]{1,0:T(8,128)(2,1)} %get-tuple-element.11) | copy-start | bytes 2359300
  175.4 3.1 %copy-start.1 = (bf16[192,2048]{1,0:T(8,128)(2,1)S(1)}, bf16[192,2048]{1,0:T(8,128)(2,1)}, u32[]{:S(2)}) copy-start(bf16[192,2048]{1,0:T(8,128)(2,1)} %get-tuple-element.12) | copy-start | bytes 2359300
  177.6 1.8 copy-start.3
  178.5 1.7 copy-start

commit v4 on v3

--- a/solution.py
+++ b/solution.py
@@ -266,7 +266,7 @@
 
     pair_wait(2)
 
-    @pl.loop(0, LOCAL_HEADS)
+    @pl.loop(0, 3)
     def _(j):
         zcopy(2, j).start()
 
@@ -362,7 +362,6 @@
         for cp in tab:
             cp.start()
 
-    gate_z()
     ones = jnp.ones((8, HEAD_DIM), F32)
 
     @pl.loop(0, LOCAL_HEADS // 2)
@@ -376,6 +375,13 @@
                 ones, prod, NT, preferred_element_type=F32, precision=lax.Precision.HIGHEST
             )
             stats[0, 1, pl.ds(j, 1), :] = delta[0:1, :]
+
+    gate_z()
+    gate_x()
+
+    @pl.loop(3, LOCAL_HEADS)
+    def _(j):
+        zcopy(2, j).start()
 
     stat_copy = remote(stats.at[0], stats.at[1], ds_s.at[0], ds_r.at[0], anti)
     stat_copy.start()
@@ -408,14 +414,13 @@
         dva[:, head(j)] = dot(p[:HALF].astype(BF), do, NN)
         for cp in out_copies(0, j):
             cp.start()
+        pl.when(j == 1)(gate_y)
+        pl.when(j == 4)(gate_tables)
 
     stat_copy.wait_recv()
 
     @pl.loop(0, LOCAL_HEADS)
     def _(j):
-        pl.when(j == 2)(gate_x)
-        pl.when(j == 4)(gate_y)
-        pl.when(j == 6)(gate_tables)
         zcopy(2, j).wait_recv()
         zcopy(3, j).wait_recv()
         q = qb[other, head(j)]

time: 182 us -> 185 us (1.016)
  Pallas kernels: 175 us -> 177 us
    pallas_call x1, Pallas kernels: 175 us -> 177 us  [shards(): pl.pallas_call(kernel, name='attention_grads', out_shape=(out_rows, out_r...]
where the time goes in v4:
time: 185 us; the launch traced here: 184 us
  Pallas kernels  177 us (96%)
  local copies, waits for them, and re-layouts  5.74 us (3%)
    pallas_call x1, Pallas kernels, shards(): pl.pallas_call(kernel, name='attention_grads', out_shape=(out_rows, out_r...  177 us
    unnamed x13, local copies, waits for them, and re-layouts  5.74 us

profile of v4, /device:TPU:71, one launch (start us, length us, event | category | flops | bytes accessed | tf_op | source)
XLA Modules:
  0.0 183.9 jit_solution(5667377499123305694)
XLA Ops:
  0.6 177.5 %attention_grads.1 = (bf16[192,2048]{1,0:T(8,128)(2,1)}, bf16[192,2048]{1,0:T(8,128)(2,1)}, bf16[192,2048]{1,0:T(8,128)(2,1)}, f32[32,4096]{1,0:T(8,128)}, f32[64,4096]{1,0:T(8,128)}) custom-call(s32[64]{0:T(128)} %ts_ref.1, s32[64]{0:T(128)} %sp_ref.1, s32[64]{0:T(128)} %ln_ref.1, bf16[192,2048]{1,0:T(8,128)(2,1)} %bitcast.8, bf16[192,2048]{1,0:T(8,128)(2,1)} %bitcast.9, ...), custom_call_target="tpu_custom_call" | custom-call | tf_op jit(solution)/shard_map/attention_grads/pallas_call | solution.py:480
  178.1 0.0 copy-start.2
  178.1 0.0 copy-start.1
  178.1 2.2 %copy.20 = bf16[1,192,2048]{2,1,0:T(8,128)(2,1)} copy(bf16[1,192,2048]{2,1,0:T(8,128)(2,1)} %bitcast.13) | data formatting | bytes 1572864
  180.3 0.0 copy-done.2
  180.3 0.0 copy-start.3
  180.3 0.9 copy.21
  181.2 0.0 copy-done.1
  181.2 0.0 copy-start
  181.2 0.9 copy.22
  182.1 0.0 copy-done.3
  182.1 0.8 copy.23
  182.9 0.0 copy-done
  182.9 1.0 copy.24
Async XLA Ops:
  178.1 2.2 %copy-start.2 = (bf16[192,2048]{1,0:T(8,128)(2,1)S(1)}, bf16[192,2048]{1,0:T(8,128)(2,1)}, u32[]{:S(2)}) copy-start(bf16[192,2048]{1,0:T(8,128)(2,1)} %get-tuple-element.11) | copy-start | bytes 2359300
  178.1 3.1 %copy-start.1 = (bf16[192,2048]{1,0:T(8,128)(2,1)S(1)}, bf16[192,2048]{1,0:T(8,128)(2,1)}, u32[]{:S(2)}) copy-start(bf16[192,2048]{1,0:T(8,128)(2,1)} %get-tuple-element.12) | copy-start | bytes 2359300
  180.3 1.8 copy-start.3
  181.2 1.7 copy-start
